TPU v7x, 32 devices: a whole 2x2x4 slice. The times are simulated.
32 devices in a mesh: rep: 2 (over y), tp: 8 (over z, x), sub: 2 (over core).
Axes of the slice: x: 2, y: 2, z: 4, core: 2. Of those that a mesh axis runs over, the one named last changes fastest.
Arguments:
- queries: bfloat16 [512, 16384], P('rep', 'tp'), parts along dimension 0, may hold values from -100 to 100
- kv_cache: bfloat16 [8, 32768, 256], P('tp', ('rep', 'sub')), parts along dimension 1, may hold values from -6 to 6, as said below
- out_proj: bfloat16 [16384, 16384], P('tp', 'sub'), may hold values from -3.5 to 3.5
- first_scales: float32 [8, 128], P(None, 'sub'), may hold values from 0.000335 to 0.00223
- second_scales: float32 [128], P('sub'), may hold values from 0.00335 to 0.0112
Outputs:
- attention_output: bfloat16 [512, 16384], P('rep', 'sub'), parts along dimension 0
There are 2 independent parts, one for each index of `rep`. A program takes and returns all parts, laid end to end along the dimension named above; an argument that names none is the same for every part. Nothing has to cross between parts.
Inputs may be any that keep to these rules, and one draw needn't show every extreme that they name: `kv_cache`: rows i and j of the first dimension are equal whenever i * 1 == j * 1.
All inputs are finite; a program needn't handle non-finite values.
Results may differ from a plain program's by a relative error of at most 0.024.
Values may be sent and summed in bfloat16 or wider, within the bound.
A program may use at most 192 MiB of HBM per device.

v0:
```python
import math

import jax
import jax.numpy as jnp
from jax import lax
from jax.sharding import PartitionSpec as P

BLK = 128


saturation = 448.0


def merged(x, axis, join):
    gathered = jax.tree.map(
        lambda a, kind: lax.all_gather(a.astype(kind), axis),
        x,
        (jnp.bfloat16, jnp.bfloat16, jnp.bfloat16),
    )

    def take(source):
        return jax.tree.map(
            lambda a, own: lax.dynamic_index_in_dim(a, source, 0, False).astype(own.dtype),
            gathered,
            x,
        )

    return lax.fori_loop(
        1, lax.axis_size(axis), lambda source, state: join(state, take(source)), take(0)
    )


def hadamard(block_size):
    indices = jnp.arange(block_size, dtype=jnp.int32)
    common_bits = jnp.bitwise_and(indices[:, None], indices[None, :])
    parity = jnp.zeros((block_size, block_size), jnp.int32)
    for bit_number in range(block_size.bit_length() - 1):
        parity = parity + jnp.bitwise_and(jnp.right_shift(common_bits, bit_number), 1)
    sign_matrix = 1 - 2 * (parity % 2)
    return sign_matrix.astype(jnp.float32) / math.sqrt(block_size)


def combine(first_part, second_part):
    first_max, first_sum, first_acc = first_part
    second_max, second_sum, second_acc = second_part
    row_max = jnp.maximum(first_max, second_max)
    first_factor = jnp.exp(first_max - row_max)
    second_factor = jnp.exp(second_max - row_max)
    row_sum = first_sum * first_factor + second_sum * second_factor
    summed = first_acc * first_factor[..., None] + second_acc * second_factor[..., None]
    return (row_max, row_sum, summed)


def shards(queries, kv_cache, out_proj, first_scales, second_scales):
    tokens = queries.shape[0]
    columns_here = out_proj.shape[1]
    head_dim = kv_cache.shape[2] // 2
    local_heads = queries.shape[1] // head_dim
    keys_here = kv_cache.shape[1]
    tp_count = lax.axis_size("tp")
    tp_place = lax.axis_index("tp")
    sub_place = lax.axis_index("sub")
    total_ctx = keys_here * lax.axis_size("sub")
    query_pos = total_ctx - tokens + jnp.arange(tokens, dtype=jnp.int32)
    key_pos = sub_place * keys_here + jnp.arange(keys_here, dtype=jnp.int32)
    allowed = key_pos[None, :] <= query_pos[:, None]
    key_rows = kv_cache[0, :, :head_dim]
    value_rows = kv_cache[0, :, head_dim:]

    def one_head(head_index):
        query_head = lax.dynamic_slice_in_dim(queries, head_index * head_dim, head_dim, 1)
        scores = lax.dot_general(
            query_head, key_rows, (((1,), (1,)), ((), ())), preferred_element_type=jnp.float32
        )
        scores = scores / math.sqrt(head_dim)
        scores = jnp.where(allowed, scores, jnp.float32(-1e30))
        row_max = jnp.max(scores, axis=1)
        weights = jnp.exp(scores - row_max[:, None])
        row_sum = jnp.sum(weights, axis=1)
        weighted = jnp.dot(
            weights.astype(jnp.bfloat16), value_rows, preferred_element_type=jnp.float32
        )
        return (row_max, row_sum, weighted)

    row_max, row_sum, weighted = lax.map(one_head, jnp.arange(local_heads, dtype=jnp.int32))
    row_max, row_sum, weighted = merged((row_max, row_sum, weighted), "sub", combine)
    attended = (
        (weighted / row_sum[..., None]).transpose(1, 0, 2).reshape(tokens, local_heads * head_dim)
    )
    attended = attended.astype(jnp.bfloat16)
    partial_value = jnp.dot(attended, out_proj, preferred_element_type=jnp.float32)
    blocks = columns_here // BLK
    rotation = hadamard(BLK)
    rotated = jnp.dot(
        partial_value.reshape(tokens * blocks, BLK), rotation, precision=lax.Precision.HIGHEST
    ).reshape(tokens, blocks, BLK)
    own_scales = lax.dynamic_index_in_dim(first_scales, tp_place, 0, keepdims=False)
    encoded = jnp.clip(rotated / own_scales[None, :, None], -saturation, saturation).astype(
        jnp.bfloat16
    )
    own_blocks = blocks // tp_count
    outgoing = encoded.reshape(tokens, tp_count, own_blocks * BLK)
    incoming = lax.all_to_all(outgoing, "tp", split_axis=1, concat_axis=1, tiled=True)
    factors = lax.dynamic_slice_in_dim(first_scales, tp_place * own_blocks, own_blocks, 1)
    summed = jnp.sum(
        incoming.reshape(tokens, tp_count, own_blocks, BLK).astype(jnp.float32)
        * factors[None, :, :, None],
        axis=1,
    )
    sum_scales = lax.dynamic_slice_in_dim(second_scales, tp_place * own_blocks, own_blocks, 0)
    requant = jnp.clip(summed / sum_scales[None, :, None], -saturation, saturation).astype(
        jnp.bfloat16
    )
    rows_here = requant.shape[0]
    decoded = requant.astype(jnp.float32) * sum_scales[None, :, None]
    unrotated = jnp.dot(decoded.reshape(-1, BLK), rotation, precision=lax.Precision.HIGHEST)
    finished = unrotated.astype(jnp.bfloat16).reshape(1, rows_here, -1)
    assembled = lax.all_gather(finished, "tp", axis=0, tiled=True)
    result = assembled.transpose(1, 0, 2).reshape(tokens, columns_here)
    return result


def solution(mesh):
    placed = (
        P("rep", "tp"),
        P("tp", ("rep", "sub"), None),
        P("tp", "sub"),
        P(None, "sub"),
        P("sub"),
    )
    return jax.shard_map(
        shards, mesh=mesh, in_specs=placed, out_specs=P("rep", "sub"), check_vma=False
    )
```

profile of v0, /device:TPU:16, one launch (start us, length us, event | category | flops | bytes accessed | tf_op | source)
XLA Modules:
  0.0 422.7 jit_solution(18140955966095789565)
XLA Ops:
  6.5 3.8 slice_bitcast_fusion
  10.4 132.2 %while.3 = (s32[]{:T(128)}, bf16[16,256]{1,0:T(8,128)(2,1)S(1)}, bf16[16,256]{1,0:T(8,128)(2,1)S(1)}, bf16[16,256,128]{2,1,0:T(8,128)(2,1)}, s32[16]{0:T(128)S(1...) while((s32[]{:T(128)}, bf16[16,256]{1,0:T(8,128)(2,1)S(1)}, ...), condition=%wide.region_3.4_spmd.clone, body=%wide.region_0.3_spmd.clone.sunk | while | flops 1090518528 | bytes 29599436 | solution.py:85
  11.8 3.2 fusion.69
  15.0 2.2 fusion.71
  20.0 3.2 fusion.69
  23.3 2.2 fusion.71
  28.3 3.3 fusion.69
  36.6 3.3 fusion.69
  39.8 2.2 fusion.71
  44.8 3.3 fusion.69
  53.1 3.3 fusion.69
  61.4 3.2 fusion.69
  69.6 3.2 fusion.69
  77.9 3.2 fusion.69
  81.1 2.2 fusion.71
  86.1 3.3 fusion.69
  94.4 3.3 fusion.69
  97.6 2.2 fusion.71
  102.7 3.2 fusion.69
  110.9 3.3 fusion.69
  119.2 3.3 fusion.69
  127.5 3.2 fusion.69
  135.7 3.3 fusion.69
  142.6 44.6 %copy.26 = bf16[8192,2048]{1,0:T(8,128)(2,1)} copy(bf16[8192,2048]{0,1:T(8,128)(2,1)} %bitcast.46) | data formatting | bytes 67108864 | tf_op jit(solution)/shard_map/dot_general | solution.py:91
  194.2 18.4 %fusion.54 = f32[256,64,128]{2,0,1:T(8,128)} fusion(bf16[256,2048,1]{0,1,2:T(8,128)(2,1)S(1)} %bitcast.50, bf16[64,128,2048]{2,1,0:T(8,128)(2,1)} %bitcast.47), kind=kOutput, calls=%fused_computation.68 | convolution fusion | flops 8589934592 | bytes 42991616 | tf_op jit(solution)/shard_map/dot_general | solution.py:91
  212.6 13.6 %clamp_convert_fusion = bf16[256,64,128]{0,2,1:T(8,128)(2,1)} fusion(f32[64]{0:T(128)S(1)} %dynamic-slice_bitcast_fusion, f32[256,64,128]{2,0,1:T(8,128)} %fusion.54), kind=kOutput, calls=%fused_computation.13 | convolution fusion | flops 3228106752 | bytes 12583168 | tf_op jit(solution)/shard_map/dot_general | solution.py:94
  226.2 6.3 %all-to-all-start = ((bf16[256,8,1024]{0,2,1:T(8,128)(2,1)}), bf16[256,8,1024]{0,2,1:T(8,128)(2,1)}, u32[]{:S(2)}, u32[]{:S(2)}) async-start(bf16[256,8,1024]{0,2,1:T(8,128)(2,1)} %bitcast.49), calls=%async_computation | async-start | bytes 8388608 | tf_op jit(solution)/shard_map/all_to_all | solution.py:103
  232.9 89.8 %all-to-all-done = bf16[256,8,1024]{0,2,1:T(8,128)(2,1)} async-done(((bf16[256,8,1024]{0,2,1:T(8,128)(2,1)}), bf16[256,8,1024]{0,2,1:T(8,128)(2,1)}, u32[]{:S(2)}, u32[]{:S(2)}) %all-to-all-start) | async-done | bytes 4194336 | tf_op jit(solution)/shard_map/all_to_all | solution.py:103
  322.8 2.9 multiply_reduce_fusion
  328.3 74.7 %all-gather.6.cloned.1.call-done = bf16[8,256,1024]{2,1,0:T(8,128)(2,1)} async-done(((bf16[1,256,1024]{2,1,0:T(8,128)(2,1)}), bf16[8,256,1024]{2,1,0:T(8,128)(2,1)}) %all-gather.6.cloned.1.call-update) | async-done | bytes 4194320 | tf_op jit(solution)/shard_map/all_gather | solution.py:118
  403.0 6.5 %copy.22 = bf16[8,256,1024]{1,2,0:T(8,128)(2,1)} copy(bf16[8,256,1024]{2,1,0:T(8,128)(2,1)} %all-gather.6.cloned.1.call-done) | data formatting | bytes 8388608 | tf_op jit(solution)/shard_map/all_gather | solution.py:118
  409.5 6.3 %copy.23 = bf16[256,8192]{1,0:T(8,128)(2,1)} copy(bf16[256,8192]{0,1:T(8,128)(2,1)} %bitcast.48) | data formatting | bytes 8388608 | tf_op jit(solution)/shard_map/reshape | solution.py:119
  (108 shorter events, 67.7 us)
Async XLA Ops:
  6.5 184.3 %copy-start = (f32[8,64]{1,0:T(8,128)S(1)}, f32[8,64]{1,0:T(8,128)}, u32[]{:S(2)}) copy-start(f32[8,64]{1,0:T(8,128)} %param.10) | copy-start | bytes 6148
  6.5 184.3 %all-gather.8.cloned.1.call-start = ((), (), s32[]{:S(2)}) async-start(), calls=%async_computation.2 | async-start | bytes 3145728 | tf_op jit(solution)/shard_map/all_gather | solution.py:16
  226.2 6.4 %copy-start.1 = (f32[64]{0:T(128)S(1)}, f32[64]{0:T(128)}, u32[]{:S(2)}) copy-start(f32[64]{0:T(128)} %param.11) | copy-start | bytes 772
  226.2 96.5 %all-to-all-start = ((bf16[256,8,1024]{0,2,1:T(8,128)(2,1)}), bf16[256,8,1024]{0,2,1:T(8,128)(2,1)}, u32[]{:S(2)}, u32[]{:S(2)}) async-start(bf16[256,8,1024]{0,2,1:T(8,128)(2,1)} %bitcast.49), calls=%async_computation | async-start | bytes 8388608 | tf_op jit(solution)/shard_map/all_to_all | solution.py:103
  232.5 170.5 %all-gather.6.cloned.1.call-start = ((), (), s32[]{:S(2)}) async-start(), calls=%async_computation.1 | async-start | bytes 4718592 | tf_op jit(solution)/shard_map/all_gather | solution.py:118
Sparse Core Ops, SparseCore 0:
  142.8 11.8 all-gather.7
  328.5 74.4 all-gather.5
where the time goes:
time: 427 us; the launch traced here: 423 us
  waiting for transfers between devices  165 us (39%)
  matrix products  121 us (28%)
  local copies, waits for them, and re-layouts  77.7 us (18%)
  other arithmetic  25.1 us (6%)
  between operations  13.5 us (3%)
  loops' own time  11.5 us (3%)
  starting transfers between devices  6.29 us (1%)
    all_to_all x1, waiting for transfers between devices, shards(): lax.all_to_all(outgoing, 'tp', split_axis=1, concat_axis=1, tiled=True)  89.8 us
    all_gather x1, waiting for transfers between devices, shards(): assembled = lax.all_gather(finished, 'tp', axis=0, tiled=True)  74.7 us
    dot_general x16, matrix products, one_head(): lax.dot_general(query_head, key_rows, (((1,), (1,)), ((), ())), preferred...  52 us
    dot_general x1, local copies, waits for them, and re-layouts, shards(): jnp.dot(attended, out_proj, preferred_element_type=jnp.float32)  44.6 us
    dot_general x16, matrix products, one_head(): jnp.dot(weights.astype(jnp.bfloat16), value_rows, preferred_element_type=...  35.4 us
    reduce_sum x16, other arithmetic, one_head(): row_sum = jnp.sum(weights, axis=1)  21.6 us
    dot_general x1, matrix products, shards(): jnp.dot(attended, out_proj, preferred_element_type=jnp.float32)  18.4 us
    dot_general x1, matrix products, shards(): jnp.dot(partial_value.reshape(tokens * blocks, BLK), rotation, precision=...  13.6 us
  transfers between devices with their start and end apart: 3, of which 2 were waited for; matrix products, arithmetic and copies ran while one was open for 11% of the time, Pallas kernels for 0%

commit v1 on v0

v1 whole, which is shorter than its diff:
```python
import functools
import math

import jax
import jax.numpy as jnp
import numpy as np
from jax import lax
from jax.experimental import pallas as pl
from jax.experimental.pallas import tpu as pltpu
from jax.sharding import PartitionSpec as P

BLK = 128
SATURATION = 448.0
MESH = pl.DeviceIdType.MESH
KEY_BLOCK = 1024


def hadamard_signs():
    index = np.arange(BLK)
    common = index[:, None] & index[None, :]
    parity = np.zeros((BLK, BLK), np.int64)
    for bit in range(BLK.bit_length() - 1):
        parity += (common >> bit) & 1
    return (1 - 2 * (parity % 2)).astype(np.float32)


def attention_kernel(n_sub, q_ref, kv_ref, o_ref, stat_ref, k2, v1):
    head = pl.program_id(0)
    tokens, dim = q_ref.shape
    keys = kv_ref.shape[0]
    step = min(KEY_BLOCK, keys)

    @pl.when(head == 0)
    def _():
        stat_ref[...] = jnp.zeros_like(stat_ref)

        @pl.loop(0, keys // step)
        def _(j):
            rows = pl.ds(pl.multiple_of(j * step, step), step)
            k2[rows, :dim] = kv_ref[rows, :dim]
            k2[rows, dim:] = kv_ref[rows, :dim]
            v1[rows, :dim] = kv_ref[rows, dim:]
            v1[rows, dim:] = jnp.ones((step, dim), jnp.bfloat16)

    scaled = q_ref[...].astype(jnp.float32) * (math.log2(math.e) / math.sqrt(dim))
    high = scaled.astype(jnp.bfloat16)
    low = (scaled - high.astype(jnp.float32)).astype(jnp.bfloat16)
    q2 = jnp.concatenate([high, low], axis=1)
    first_key = lax.axis_index("sub") * keys
    first_query = keys * n_sub - tokens

    def scores_of(j):
        block = lax.dot_general(
            q2,
            k2[j * step : (j + 1) * step, :],
            (((1,), (1,)), ((), ())),
            preferred_element_type=jnp.float32,
        )
        if (j + 1) * step <= keys - tokens:
            return block
        wide = min(tokens, step)
        key_pos = first_key + (j + 1) * step - wide + lax.broadcasted_iota(jnp.int32, (tokens, wide), 1)
        query_pos = first_query + lax.broadcasted_iota(jnp.int32, (tokens, wide), 0)
        masked = jnp.where(key_pos <= query_pos, block[:, step - wide :], jnp.float32(-1e30))
        return masked if wide == step else jnp.concatenate([block[:, : step - wide], masked], axis=1)

    count = keys // step
    ahead = scores_of(0)
    row_max = None
    total = None
    for j in range(count):
        scores = ahead
        if j + 1 < count:
            ahead = scores_of(j + 1)
        block_max = jnp.max(scores, axis=1, keepdims=True)
        new_max = block_max if row_max is None else jnp.maximum(row_max, block_max)
        weights = jnp.exp2((scores - new_max).astype(jnp.bfloat16))
        product = jnp.dot(weights, v1[j * step : (j + 1) * step, :], preferred_element_type=jnp.float32)
        total = product if total is None else total * jnp.exp2(row_max - new_max) + product
        row_max = new_max
    row_sum = total[:, dim:]
    o_ref[...] = (total[:, :dim] / row_sum).astype(o_ref.dtype)
    level = row_max + jnp.log2(row_sum)
    lane = lax.broadcasted_iota(jnp.int32, stat_ref.shape, 1)
    stat_ref[...] = jnp.where(lane == head, level, stat_ref[...])


def attention(n_sub, queries, kv):
    tokens, width = queries.shape
    keys, both = kv.shape
    dim = both // 2
    heads = width // dim
    return pl.pallas_call(
        functools.partial(attention_kernel, n_sub),
        out_shape=(
            jax.ShapeDtypeStruct((tokens, width), jnp.bfloat16),
            jax.ShapeDtypeStruct((tokens, BLK), jnp.float32),
        ),
        grid=(heads,),
        in_specs=[
            pl.BlockSpec((tokens, dim), lambda h: (0, h)),
            pl.BlockSpec((keys, both), lambda h: (0, 0)),
        ],
        out_specs=(
            pl.BlockSpec((tokens, dim), lambda h: (0, h)),
            pl.BlockSpec((tokens, BLK), lambda h: (0, 0)),
        ),
        scratch_shapes=[
            pltpu.VMEM((keys, both), jnp.bfloat16),
            pltpu.VMEM((keys, both), jnp.bfloat16),
        ],
        compiler_params=pltpu.CompilerParams(
            dimension_semantics=("arbitrary",), vmem_limit_bytes=48 * 2**20
        ),
    )(queries, kv)


HALVES = 2
SLOTS = 3


def project_kernel(
    n_tp,
    o_ref,
    stat_ref,
    w_ref,
    s1_ref,
    s2_ref,
    h_ref,
    out_ref,
    o_in,
    stat_in,
    att,
    wbuf,
    x_out,
    x_in,
    own,
    z_out,
    z_in,
    w_sem,
    sub_send,
    sub_recv,
    xs_sem,
    xr_sem,
    zs_sem,
    zr_sem,
    gs_sem,
    gr_sem,
    fs_sem,
    fr_sem,
):
    tokens, width = o_ref.shape
    heads = width // BLK
    columns = w_ref.shape[1]
    nz = n_tp // 2
    part = columns // n_tp
    tile = min(256, part)
    half = tokens // HALVES
    me = lax.axis_index("tp")
    sub = lax.axis_index("sub")
    z, x = me // 2, me % 2
    other_x = 1 - x
    partner = z * 2 + other_x

    def peer(k):
        return lax.rem(z + 1 + k, nz)

    def back(k):
        return lax.rem(z - 1 - k + 2 * nz, nz)

    def cols(owner):
        return pl.ds(pl.multiple_of(owner * part, part), part)

    order = [peer(k) * 2 + other_x for k in range(nz)] + [peer(k) * 2 + x for k in range(nz)]

    def fetch(i):
        return pltpu.make_async_copy(w_ref.at[:, cols(order[i])], wbuf.at[i % SLOTS], w_sem.at[i % SLOTS])

    for i in range(min(SLOTS, 2 * nz)):
        fetch(i).start()

    barrier = pltpu.get_barrier_semaphore()
    pl.semaphore_signal(barrier, inc=1, device_id={"sub": 1 - sub}, device_id_type=MESH)
    pl.semaphore_signal(barrier, inc=1, device_id={"tp": partner}, device_id_type=MESH)
    for k in range(nz - 1):
        pl.semaphore_signal(barrier, inc=1, device_id={"tp": peer(k) * 2 + x}, device_id_type=MESH)
    pl.semaphore_wait(barrier, nz + 1)

    def remote(src, dst, send, recv, where):
        return pltpu.make_async_remote_copy(
            src_ref=src, dst_ref=dst, send_sem=send, recv_sem=recv, device_id=where, device_id_type=MESH
        )

    to_sub = [
        remote(o_ref, o_in, sub_send.at[0], sub_recv.at[0], {"sub": 1 - sub}),
        remote(stat_ref, stat_in, sub_send.at[1], sub_recv.at[1], {"sub": 1 - sub}),
    ]
    for copy in to_sub:
        copy.start()
    for copy in to_sub:
        copy.wait()

    share = 1.0 / (1.0 + jnp.exp2(stat_in[...] - stat_ref[...]))
    for h in range(heads):
        here = slice(h * BLK, (h + 1) * BLK)
        mine = share[:, h : h + 1]
        theirs = o_in[:, here].astype(jnp.float32)
        att[:, here] = (theirs + (o_ref[:, here].astype(jnp.float32) - theirs) * mine).astype(att.dtype)

    signs = h_ref[...]
    stacked = jnp.concatenate([signs, signs], axis=0)
    norm = 1.0 / math.sqrt(BLK)

    def chunk(i, write):
        fetch(i).wait()
        base = order[i] * part
        slot = i % SLOTS

        @pl.loop(0, part // tile)
        def _(t):
            here = pl.ds(pl.multiple_of(t * tile, tile), tile)
            value = jnp.dot(att[...], wbuf[slot, :, here], preferred_element_type=jnp.float32)
            for b in range(tile // BLK):
                piece = value[:, b * BLK : (b + 1) * BLK]
                high = piece.astype(jnp.bfloat16)
                low = (piece - high.astype(jnp.float32)).astype(jnp.bfloat16)
                turned = jnp.dot(
                    jnp.concatenate([high, low], axis=1), stacked, preferred_element_type=jnp.float32
                )
                at = pl.multiple_of(t * tile + b * BLK, BLK)
                limit = SATURATION * s1_ref[:, pl.ds(pl.multiple_of(base + at, BLK), BLK)]
                write(pl.ds(at, BLK), jnp.minimum(jnp.maximum(turned * norm, -limit), limit))

        if i + SLOTS < 2 * nz:
            fetch(i + SLOTS).start()

    def rows(h):
        return pl.ds(h * half, half)

    def x_copy(h, k):
        return remote(
            x_out.at[k, rows(h)], x_in.at[k, rows(h)], xs_sem.at[h, k], xr_sem.at[h, k], {"tp": partner}
        )

    def z_copy(h, k):
        return remote(
            z_out.at[k, rows(h)], z_in.at[k, rows(h)], zs_sem.at[h, k], zr_sem.at[h, k], {"tp": peer(k) * 2 + x}
        )

    def g_copy(h, k):
        place = out_ref.at[rows(h), cols(me)]
        return remote(place, place, gs_sem.at[h, k], gr_sem.at[h, k], {"tp": peer(k) * 2 + x})

    def g_arrival(h, k):
        place = out_ref.at[rows(h), cols(back(k) * 2 + x)]
        return remote(place, place, gs_sem.at[h, k], gr_sem.at[h, k], {"tp": peer(k) * 2 + x})

    def f_copy(h, k):
        place = out_ref.at[rows(h), cols(back(k) * 2 + x)]
        return remote(place, place, fs_sem.at[h, k], fr_sem.at[h, k], {"tp": partner})

    def f_arrival(h, k):
        place = out_ref.at[rows(h), cols(back(k) * 2 + other_x)]
        return remote(place, place, fs_sem.at[h, k], fr_sem.at[h, k], {"tp": partner})

    for k in range(nz):

        def to_partner(here, value, k=k):
            x_out[k, :, here] = value.astype(x_out.dtype)

        chunk(k, to_partner)
        x_copy(0, k).start()
    for h in range(1, HALVES):
        for k in range(nz):
            x_copy(h, k).start()
    for k in range(nz):

        def to_own(here, value, k=k):
            own[k, :, here] = value

        chunk(nz + k, to_own)

    def pair_sums(h):
        for k in range(nz):
            x_copy(h, k).wait_recv()
            value = own[k, rows(h), :] + x_in[k, rows(h), :].astype(jnp.float32)
            if k < nz - 1:
                z_out[k, rows(h), :] = value.astype(z_out.dtype)
                z_copy(h, k).start()
            else:
                own[k, rows(h), :] = value

    def finish(h):
        for k in range(nz - 1):
            z_copy(h, k).wait_recv()
        for b in range(part // BLK):
            here = slice(b * BLK, (b + 1) * BLK)
            value = own[nz - 1, rows(h), here]
            for k in range(nz - 1):
                value = value + z_in[k, rows(h), here].astype(jnp.float32)
            place = pl.ds(pl.multiple_of(me * part + b * BLK, BLK), BLK)
            scale = s2_ref[:, place]
            coded = jnp.minimum(jnp.maximum(value / scale, -SATURATION), SATURATION).astype(jnp.bfloat16)
            plain = jnp.dot(coded, signs, preferred_element_type=jnp.float32) * (scale * norm)
            out_ref[rows(h), place] = plain.astype(out_ref.dtype)
        for k in range(nz - 1):
            g_copy(h, k).start()
        f_copy(h, nz - 1).start()

    def forward(h):
        for k in range(nz - 1):
            g_arrival(h, k).wait_recv()
            f_copy(h, k).start()

    pair_sums(0)
    finish(0)
    for h in range(1, HALVES):
        pair_sums(h)
        forward(h - 1)
        finish(h)
    forward(HALVES - 1)
    for h in range(HALVES):
        for k in range(nz):
            f_arrival(h, k).wait_recv()
    for h in range(HALVES):
        for k in range(nz):
            x_copy(h, k).wait_send()
            f_copy(h, k).wait_send()
            if k < nz - 1:
                z_copy(h, k).wait_send()
                g_copy(h, k).wait_send()


def project(n_tp, o, stat, w, s1, s2, signs):
    tokens, width = o.shape
    columns = w.shape[1]
    nz = n_tp // 2
    part = columns // n_tp
    vmem = pl.BlockSpec(memory_space=pltpu.VMEM)
    sem = pltpu.SemaphoreType.DMA
    return pl.pallas_call(
        functools.partial(project_kernel, n_tp),
        out_shape=jax.ShapeDtypeStruct((tokens, columns), jnp.bfloat16),
        in_specs=[vmem, vmem, pl.BlockSpec(memory_space=pl.ANY), vmem, vmem, vmem],
        out_specs=vmem,
        scratch_shapes=[
            pltpu.VMEM((tokens, width), jnp.bfloat16),
            pltpu.VMEM((tokens, BLK), jnp.float32),
            pltpu.VMEM((tokens, width), jnp.bfloat16),
            pltpu.VMEM((SLOTS, width, part), jnp.bfloat16),
            pltpu.VMEM((nz, tokens, part), jnp.bfloat16),
            pltpu.VMEM((nz, tokens, part), jnp.bfloat16),
            pltpu.VMEM((nz, tokens, part), jnp.float32),
            pltpu.VMEM((nz - 1, tokens, part), jnp.bfloat16),
            pltpu.VMEM((nz - 1, tokens, part), jnp.bfloat16),
            sem((SLOTS,)),
            sem((2,)),
            sem((2,)),
        ]
        + [sem((HALVES, nz))] * 8,
        compiler_params=pltpu.CompilerParams(
            collective_id=0, has_side_effects=True, vmem_limit_bytes=56 * 2**20
        ),
    )(o, stat, w, s1, s2, signs)


def shards(n_tp, n_sub, queries, kv_cache, out_proj, first_scales, second_scales):
    o, stat = attention(n_sub, queries, kv_cache[0])
    own_scales = lax.dynamic_index_in_dim(first_scales, lax.axis_index("tp"), 0, keepdims=True)
    s1 = jnp.repeat(own_scales, BLK, axis=1)
    s2 = jnp.repeat(second_scales[None, :], BLK, axis=1)
    signs = jnp.asarray(hadamard_signs(), jnp.bfloat16)
    return project(n_tp, o, stat, out_proj, s1, s2, signs)


def solution(mesh):
    placed = (
        P("rep", "tp"),
        P("tp", ("rep", "sub"), None),
        P("tp", "sub"),
        P(None, "sub"),
        P("sub"),
    )
    return jax.shard_map(
        functools.partial(shards, mesh.shape["tp"], mesh.shape["sub"]),
        mesh=mesh,
        in_specs=placed,
        out_specs=P("rep", "sub"),
        check_vma=False,
    )
```

time: 427 us -> 197 us (0.46)
  Pallas kernels: 0 us -> 187 us
  waiting for transfers between devices: 165 us -> 0 us
  matrix products: 121 us -> 0 us
  local copies, waits for them, and re-layouts: 77.7 us -> 10.2 us
  other arithmetic: 25.1 us -> 0 us
  between operations: 13.5 us -> 0.03 us
  loops' own time: 11.5 us -> 0 us
  starting transfers between devices: 6.29 us -> 0 us
    pallas_call x0 -> x2, Pallas kernels: none -> 187 us  [the longest x1 140 us: project(): pl.pallas_call(functools.partial(project_kernel, n_tp), out_shape=jax.Sha...]
    dot_general x35 -> x0, matrix products: 121 us -> none  [the longest x16 52 us: one_head(): lax.dot_general(query_head, key_rows, (((1,), (1,)), ((), ())), preferred...]
    all_to_all x1 -> x0, waiting for transfers between devices: 89.8 us -> none  [shards(): lax.all_to_all(outgoing, 'tp', split_axis=1, concat_axis=1, tiled=True)]
    all_gather x2 -> x0, waiting for transfers between devices: 74.7 us -> none  [the longest x1 74.7 us: shards(): assembled = lax.all_gather(finished, 'tp', axis=0, tiled=True)]
    dot_general x1 -> x0, local copies, waits for them, and re-layouts: 44.6 us -> none  [shards(): jnp.dot(attended, out_proj, preferred_element_type=jnp.float32)]
    reduce_sum x17 -> x0, other arithmetic: 24.5 us -> none  [the longest x16 21.6 us: one_head(): row_sum = jnp.sum(weights, axis=1)]
    dynamic_slice x20 -> x1, local copies, waits for them, and re-layouts: 12.6 us -> 0.01 us  [shards(): lax.dynamic_index_in_dim(first_scales, lax.axis_index('tp'), 0, keepdims=...]
    another operation x1 -> x0, loops' own time: 11.5 us -> none  [shards(): lax.map(one_head, jnp.arange(local_heads, dtype=jnp.int32))]
  transfers between devices with their start and end apart: 3 -> 0, of which waited for: 2 -> 0; matrix products, arithmetic and copies ran while one was open for 11% -> 0% of each run, Pallas kernels for 0% -> 0%
where the time goes in v1:
time: 197 us
  Pallas kernels  187 us (95%)
  local copies, waits for them, and re-layouts  10.2 us (5%)
    pallas_call x1, Pallas kernels, project(): pl.pallas_call(functools.partial(project_kernel, n_tp), out_shape=jax.Sha...  140 us
    pallas_call x1, Pallas kernels, attention(): pl.pallas_call(functools.partial(attention_kernel, n_sub), out_shape=(jax...  47.1 us
    unnamed x9, local copies, waits for them, and re-layouts  8.16 us

profile of v1, /device:TPU:16, one launch (start us, length us, event | category | flops | bytes accessed | tf_op | source)
XLA Modules:
  0.0 196.9 jit_solution(14134032995513701329)
XLA Ops:
  0.0 0.0 copy-start
  0.0 0.7 copy-done
  0.7 0.7 broadcast_in_dim.11
  1.4 1.3 broadcast_in_dim.13
  2.7 0.0 copy-start.1
  2.7 1.2 copy-done.1
  4.0 47.1 %shard_map.64 = (bf16[256,2048]{1,0:T(8,128)(2,1)S(1)}, f32[256,128]{1,0:T(8,128)S(1)}) custom-call(bf16[256,2048]{1,0:T(8,128)(2,1)S(1)} %copy-done.1, bf16[8192,256]{1,0:T(8,128)(2,1)} %bitcast.5), custom_call_target="tpu_custom_call" | custom-call | tf_op jit(solution)/shard_map/pallas_call | solution.py:93
  51.0 0.0 copy-start.2
  51.0 1.0 copy-done.2
  52.0 0.0 copy-start.3
  52.0 0.6 copy-done.3
  52.6 139.6 %shard_map.65 = bf16[256,8192]{1,0:T(8,128)(2,1)} custom-call(bf16[256,2048]{1,0:T(8,128)(2,1)} %copy-done.2, f32[256,128]{1,0:T(8,128)} %copy-done.3, bf16[2048,8192]{1,0:T(8,128)(2,1)} %w_ref.1, f32[1,8192]{1,0:T(1,128)} %bitcast.6, f32[1,8192]{1,0:T(1,128)} %bitcast.7, bf16[128,128]{1,0:T(8,128)(2,1)} %constant.14.clone.h_ref), custom_call_target="tpu_custom_call" | custom-call | tf_op jit(solution)/shard_map/pallas_call | solution.py:341
  192.2 4.6 %copy.8 = bf16[256,8192]{1,0:T(8,128)(2,1)} copy(bf16[256,8192]{1,0:T(8,128)(2,1)} %shard_map.65) | data formatting | bytes 8388608
  (1 shorter events, 0.0 us)
Async XLA Ops:
  0.0 0.7 copy-start
  2.7 1.2 copy-start.1
  51.0 1.0 copy-start.2
  52.0 0.6 copy-start.3
